TPU v7x, 32 devices: a whole 2x2x4 slice. The times are simulated.
32 devices in a mesh: dp: 16 (over z, x, core), tensor: 2 (over y).
Axes of the slice: x: 2, y: 2, z: 4, core: 2. Of those that a mesh axis runs over, the one named last changes fastest.
Arguments:
- gate_pre: bfloat16 [8192, 13312], P('dp', 'tensor'), may hold values from -6 to 6
- up_pre: bfloat16 [8192, 13312], P('dp', 'tensor'), may hold values from -6 to 6
- out_grad: bfloat16 [8192, 5120], P('dp', 'tensor'), may hold values from -0.06591797 to 0.06591797
- master: float32 [5120, 13312], P('dp', 'tensor'), may hold values from -6 to 6
- moment_one: float32 [5120, 13312], P('dp', 'tensor'), may hold values from -3 to 3
- moment_two: float32 [5120, 13312], P('dp', 'tensor'), may hold values from 0.05 to 1
Outputs:
- master_new: float32 [5120, 13312], P('dp', 'tensor')
- moment_one_new: float32 [5120, 13312], P('dp', 'tensor')
- moment_two_new: float32 [5120, 13312], P('dp', 'tensor')
- serving: bfloat16 [5120, 13312], P(('dp', 'tensor'))
All inputs are finite; a program needn't handle non-finite values.
Results may differ from a plain program's by a relative error of at most 0.006.
Values may be sent and summed in bfloat16 or wider, within the bound.
A program may use at most 320 MiB of HBM per device.

v0:
```python
import jax
import jax.numpy as jnp
from jax import lax
from jax.sharding import PartitionSpec as P


def on_device(gate_pre, up_pre, out_grad, master, moment_one, moment_two):
    hidden = (jax.nn.silu(gate_pre.astype(jnp.float32)) * up_pre.astype(jnp.float32)).astype(
        jnp.bfloat16
    )
    contract = (((0,), (0,)), ((), ()))
    full_grad = lax.all_gather(out_grad, "tensor", axis=1, tiled=True)
    grad = lax.psum_scatter(
        lax.dot_general(full_grad, hidden, contract, preferred_element_type=jnp.float32).astype(
            jnp.bfloat16
        ),
        "dp",
        scatter_dimension=0,
        tiled=True,
    ).astype(jnp.float32)
    moment_one_new = 0.9 * moment_one + 0.1 * grad
    moment_two_new = 0.95 * moment_two + 0.05 * grad * grad
    first = moment_one_new / (1.0 - 0.9**20)
    second = moment_two_new / (1.0 - 0.95**20)
    master_new = master - 0.01 * (first / (jnp.sqrt(second) + 1e-08) + 0.1 * master)
    serving = lax.all_to_all(
        master_new.astype(jnp.bfloat16), "tensor", split_axis=0, concat_axis=1, tiled=True
    )
    return (master_new, moment_one_new, moment_two_new, serving)


def solution(mesh):
    placed = (
        P("dp", "tensor"),
        P("dp", "tensor"),
        P("dp", "tensor"),
        P("dp", "tensor"),
        P("dp", "tensor"),
        P("dp", "tensor"),
    )
    return jax.shard_map(
        on_device,
        mesh=mesh,
        in_specs=placed,
        out_specs=(
            P("dp", "tensor"),
            P("dp", "tensor"),
            P("dp", "tensor"),
            P(("dp", "tensor"), None),
        ),
        check_vma=False,
    )
```

profile of v0, /device:TPU:0, one launch (start us, length us, event | category | flops | bytes accessed | tf_op | source)
XLA Modules:
  0.0 937.1 jit_solution(8300616853658575136)
XLA Ops:
  7.2 0.0 all-gather.2.cloned.1.call-start
  7.2 0.7 all-gather.2.cloned.1.call-update
  7.9 0.0 reduce-scatter.4.cloned.1.call-start
  7.9 72.9 %all-gather.2.cloned.1.call-done = bf16[512,5120]{1,0:T(8,128)(2,1)} async-done(((bf16[512,2560]{1,0:T(8,128)(2,1)}), bf16[512,5120]{1,0:T(8,128)(2,1)}) %all-gather.2.cloned.1.call-update) | async-done | bytes 5242896 | tf_op jit(solution)/shard_map/all_gather | solution.py:12
  80.8 45.8 %convert_bitcast_fusion = bf16[5120,6656]{0,1:T(8,128)(2,1)} fusion(bf16[512,5120]{1,0:T(8,128)(2,1)} %all-gather.2.cloned.1.call-done, bf16[512,6656]{1,0:T(8,128)(2,1)} %param.7, bf16[512,6656]{1,0:T(8,128)(2,1)} %param.6), kind=kOutput, calls=%fused_computation | convolution fusion | flops 34957950976 | bytes 87031808 | tf_op jit(solution)/shard_map/dot_general | solution.py:14
  126.6 80.0 %copy.37 = bf16[5120,6656]{1,0:T(8,128)(2,1)} copy(bf16[5120,6656]{0,1:T(8,128)(2,1)} %convert_bitcast_fusion) | data formatting | bytes 136314880
  206.6 0.0 reduce-scatter.4.cloned.1.call-update
  206.6 649.0 %reduce-scatter.4.cloned.1.call-done = bf16[320,6656]{1,0:T(8,128)(2,1)} async-done(((bf16[5120,6656]{1,0:T(8,128)(2,1)}), bf16[320,6656]{1,0:T(8,128)(2,1)}) %reduce-scatter.4.cloned.1.call-update) | async-done | bytes 4259856 | tf_op jit(solution)/shard_map/reduce_scatter | solution.py:13
  855.7 19.6 %fusion.10 = (bf16[320,6656]{1,0:T(8,128)(2,1)}, f32[320,6656]{1,0:T(8,128)}, f32[320,6656]{1,0:T(8,128)}, f32[320,6656]{1,0:T(8,128)}) fusion(f32[320,6656]{1,0:T(8,128)} %param.9, bf16[320,6656]{1,0:T(8,128)(2,1)} %reduce-scatter.4.cloned.1.call-done, f32[320,6656]{1,0:T(8,128)} %param.10, f32[320,6656]{1,0:T(8,128)} %param.11), kind=kLoop, calls=%fused_computation.15 | loop fusion | flops 36208640 | bytes 59637760 | tf_op jit(solution)/shard_map/convert_element_type | solution.py:27
  875.3 52.5 %all_to_all.19 = bf16[2,160,6656]{2,1,0:T(8,128)(2,1)S(1)} all-to-all(bf16[2,160,6656]{2,1,0:T(8,128)(2,1)} %bitcast.10), channel_id=1, replica_groups=mesh['dp'=16,'tensor'=2] {'tensor'}, dimensions={0} | all-to-all | bytes 8519680 | tf_op jit(solution)/shard_map/all_to_all | solution.py:26
  927.7 2.5 copy.39
Async XLA Ops:
  7.2 73.7 %all-gather.2.cloned.1.call-start = ((), (), s32[]{:S(2)}) async-start(), calls=%async_computation.2 | async-start | bytes 7864320 | tf_op jit(solution)/shard_map/all_gather | solution.py:12
  7.9 847.8 %reduce-scatter.4.cloned.1.call-start = ((), (), s32[]{:S(2)}) async-start(), calls=%async_computation.3 | async-start | bytes 72417280 | tf_op jit(solution)/shard_map/reduce_scatter | solution.py:13
Sparse Core Ops, SparseCore 0:
  9.5 71.2 all-gather.1
  206.8 648.8 reduce-scatter.3
where the time goes:
time: 939 us; the launch traced here: 937 us
  waiting for transfers between devices  723 us (77%)
  local copies, waits for them, and re-layouts  82.5 us (9%)
  blocking collectives  52.5 us (6%)
  matrix products  45.8 us (5%)
  other arithmetic  19.6 us (2%)
  between operations  14 us (1%)
    reduce_scatter x1, waiting for transfers between devices, on_device(): lax.psum_scatter(lax.dot_general(full_grad, hidden, contract, preferred_e...  649 us
    unnamed x1, local copies, waits for them, and re-layouts  80 us
    all_gather x1, waiting for transfers between devices, on_device(): full_grad = lax.all_gather(out_grad, 'tensor', axis=1, tiled=True)  72.9 us
    all_to_all x1, blocking collectives, on_device(): lax.all_to_all(master_new.astype(jnp.bfloat16), 'tensor', split_axis=0, c...  52.5 us
    dot_general x1, matrix products, on_device(): lax.dot_general(full_grad, hidden, contract, preferred_element_type=jnp.f...  45.8 us
    convert_element_type x1, other arithmetic, on_device(): master_new.astype(jnp.bfloat16)  19.6 us
  transfers between devices with their start and end apart: 2, of which 2 were waited for; matrix products, arithmetic and copies ran while one was open for 0% of the time, Pallas kernels for 0%

commit v1 on v0

v1 whole, which is shorter than its diff:
```python
import functools

import jax
import jax.numpy as jnp
from jax import lax
from jax.experimental import pallas as pl
from jax.experimental.pallas import tpu as pltpu
from jax.sharding import PartitionSpec as P

MESH = pl.DeviceIdType.MESH
GROUP = 4
HID_SLOTS = 4
RECV_SLOTS = 3
EXTRA = 1
FIRST = 1.0 / (1.0 - 0.9**20)
SECOND = 1.0 / (1.0 - 0.95**20)


def kernel(
    n_dp,
    n_ten,
    width,
    gate,
    up,
    cot,
    master,
    one,
    two,
    master_out,
    one_out,
    two_out,
    serving,
    cot_all,
    gates,
    ups,
    hid,
    part,
    inc,
    outg,
    opt_in,
    opt_out,
    served,
    cot_send,
    cot_recv,
    fwd_send,
    fwd_recv,
    own_sem,
    act_sem,
    hid_send,
    hid_recv,
    hid_free,
    sum_send,
    sum_recv,
    sum_free,
    opt_sem,
    res_sem,
    srv_send,
    srv_recv,
    srv_own,
):
    tokens, hidden_cols = gate.shape
    rows = master.shape[0]
    n = hidden_cols // width
    ranks = n_dp // GROUP
    per = ranks // n_ten
    part_slots = part.shape[0]
    last = ranks - 1

    me = lax.axis_index("dp")
    ten = lax.axis_index("tensor")
    rank = lax.div(me, GROUP)
    g = lax.rem(me, GROUP)
    sib = me + 1 - 2 * lax.rem(g, 2)
    far = me + 2 - 4 * lax.div(g, 2)
    g_far = g + 2 - 4 * lax.div(g, 2)
    peers = [rank * GROUP + lax.rem(g + d, GROUP) for d in range(1, GROUP)]
    partners = [lax.rem(ten + d, n_ten) for d in range(1, n_ten)]
    below = me - GROUP
    above = me + GROUP

    barrier = pltpu.get_barrier_semaphore()
    for peer in peers:
        pl.semaphore_signal(barrier, inc=1, device_id=(peer, ten), device_id_type=MESH)
    for partner in partners:
        pl.semaphore_signal(barrier, inc=1, device_id=(me, partner), device_id_type=MESH)
    for step in (1, ranks - 1):
        other = lax.rem(rank + step, ranks) * GROUP + g
        pl.semaphore_signal(barrier, inc=1, device_id=(other, ten), device_id_type=MESH)
    pl.semaphore_wait(barrier, len(peers) + len(partners) + 2)

    def cols(k):
        return pl.ds(pl.multiple_of(k * width, width), width)

    def toks(who):
        return pl.ds(pl.multiple_of(who * tokens, tokens), tokens)

    def remote(src, dst, send, recv, dp, tensor):
        return pltpu.make_async_remote_copy(
            src_ref=src,
            dst_ref=dst,
            send_sem=send,
            recv_sem=recv,
            device_id=(dp, tensor),
            device_id_type=MESH,
        )

    def cot_here(who):
        return cot_all.at[pl.ds(ten * per, per), :, toks(who)]

    def cot_out(d):
        to = lax.rem(g + d, GROUP)
        return remote(
            cot.at[:, to], cot_here(g), cot_send.at[d - 1], cot_recv.at[d - 1],
            rank * GROUP + to, ten,
        )

    def cot_fwd(d, e):
        src = cot.at[:, g] if d == 0 else cot_here(lax.rem(g + GROUP - d, GROUP))
        return remote(
            src, cot_here(lax.rem(g + GROUP - d, GROUP)),
            fwd_send.at[e - 1, d], fwd_recv.at[e - 1, d], me, lax.rem(ten + e, n_ten),
        )

    def own_cot():
        return pltpu.make_async_copy(cot.at[:, g], cot_here(g), own_sem)

    def acts(k):
        s = lax.rem(k, 2)
        return (
            pltpu.make_async_copy(gate.at[:, cols(k)], gates.at[s], act_sem.at[0, s]),
            pltpu.make_async_copy(up.at[:, cols(k)], ups.at[s], act_sem.at[1, s]),
        )

    def opts(k):
        s = lax.rem(k, 2)
        return [
            pltpu.make_async_copy(ref.at[:, cols(k)], opt_in.at[s, j], opt_sem.at[j, s])
            for j, ref in enumerate((master, one, two))
        ]

    def results(k):
        s = lax.rem(k, 2)
        return [
            pltpu.make_async_copy(opt_out.at[s, j], ref.at[:, cols(k)], res_sem.at[j, s])
            for j, ref in enumerate((master_out, one_out, two_out))
        ]

    def hid_copy(k, which):
        s = lax.rem(k, HID_SLOTS)
        block = hid.at[s, toks(g_far if which == 2 else g)]
        to = far if which == 1 else sib
        return remote(block, block, hid_send.at[which, s], hid_recv.at[which, s], to, ten)

    def sum_copy(k, way, t):
        s = lax.rem(k, 2)
        e = lax.rem(k, RECV_SLOTS)
        return remote(
            outg.at[way, s, t], inc.at[way, e, t], sum_send.at[way, s, t],
            sum_recv.at[way, e, t], above if way == 0 else below, ten,
        )

    def srv_cols(k):
        start = ten * hidden_cols + k * width
        return pl.ds(pl.multiple_of(start, width), width)

    def srv_local(k):
        s = lax.rem(k, 2)
        return pltpu.make_async_copy(served.at[s, ten], serving.at[:, srv_cols(k)], srv_own.at[s])

    def srv_copy(k, d):
        s = lax.rem(k, 2)
        to = lax.rem(ten + d, n_ten)
        return remote(
            served.at[s, to], serving.at[:, srv_cols(k)], srv_send.at[d - 1, s],
            srv_recv.at[d - 1], me, to,
        )

    for d in range(1, GROUP):
        cot_out(d).start()
    for e in range(1, n_ten):
        cot_fwd(0, e).start()
    own_cot().start()
    for copy in acts(0):
        copy.start()
    for copy in opts(0):
        copy.start()

    def step(i, carry):
        @pl.when(i < n)
        def _():
            s = lax.rem(i, HID_SLOTS)
            q = lax.rem(i, 2)
            for copy in acts(i):
                copy.wait()

            @pl.when(i + 1 < n)
            def _():
                for copy in acts(i + 1):
                    copy.start()

            def rows_of(j, c):
                piece = pl.ds(pl.multiple_of(j * 64, 64), 64)
                v = gates[q, piece].astype(jnp.float32)
                u = ups[q, piece].astype(jnp.float32)
                value = (0.5 * v) * (1.0 + jnp.tanh(0.5 * v)) * u
                place = pl.ds(pl.multiple_of(g * tokens + j * 64, 64), 64)
                hid[s, place] = value.astype(jnp.bfloat16)
                return c

            lax.fori_loop(0, tokens // 64, rows_of, 0)

            @pl.when(i >= HID_SLOTS)
            def _():
                pl.semaphore_wait(hid_free.at[0], 1)
                pl.semaphore_wait(hid_free.at[1], 1)

            hid_copy(i, 1).start()
            hid_copy(i, 0).start()

        @pl.when(i == 0)
        def _():
            for d in range(1, GROUP):
                cot_out(d).wait_recv()
                for e in range(1, n_ten):
                    cot_fwd(d, e).start()

        b = i - 1

        @pl.when((b >= 0) & (b < n))
        def _():
            hid_copy(b, 1).wait_recv()
            hid_copy(b, 2).start()

        c = i - 2

        @pl.when(c == 0)
        def _():
            own_cot().wait()
            for d in range(GROUP):
                for e in range(1, n_ten):
                    cot_fwd(d, e).wait()
            for d in range(1, GROUP):
                cot_out(d).wait_send()

        @pl.when((c >= 0) & (c < n))
        def _():
            s = lax.rem(c, HID_SLOTS)
            hid_copy(c, 0).wait_recv()
            hid_copy(c, 2).wait_recv()

            def product(t, carry):
                part[lax.rem(c, part_slots), t] = jnp.dot(
                    cot_all[t], hid[s], preferred_element_type=jnp.float32
                )
                return carry

            lax.fori_loop(0, ranks, product, 0)
            for which in range(3):
                hid_copy(c, which).wait_send()

            @pl.when(c + HID_SLOTS < n)
            def _():
                pl.semaphore_signal(
                    hid_free.at[0], inc=1, device_id=(sib, ten), device_id_type=MESH
                )
                pl.semaphore_signal(
                    hid_free.at[1], inc=1, device_id=(far, ten), device_id_type=MESH
                )

        for way in (0, 1):
            hops = rank if way == 0 else last - rank
            k = i - 2 - hops
            source = below if way == 0 else above

            @pl.when((k >= 0) & (k < n))
            def _(way=way, hops=hops, k=k, source=source):
                ps = lax.rem(k, part_slots)
                es = lax.rem(k, RECV_SLOTS)
                qs = lax.rem(k, 2)

                def one_target(t, carry):
                    ahead = (t > rank) if way == 0 else (t < rank)

                    @pl.when((hops > 0) & (ahead | (t == rank)))
                    def _():
                        sum_copy(k, way, t).wait_recv()

                    @pl.when(ahead)
                    def _():
                        @pl.when(k >= 2)
                        def _():
                            sum_copy(k, way, t).wait_send()

                        @pl.when(hops > 0)
                        def _():
                            def rows_of(j, c):
                                piece = pl.ds(pl.multiple_of(j * 32, 32), 32)
                                value = part[ps, t, piece] + inc[way, es, t, piece].astype(
                                    jnp.float32
                                )
                                outg[way, qs, t, piece] = value.astype(jnp.bfloat16)
                                return c

                            lax.fori_loop(0, rows // 32, rows_of, 0)

                        @pl.when(hops == 0)
                        def _():
                            def rows_of(j, c):
                                piece = pl.ds(pl.multiple_of(j * 32, 32), 32)
                                outg[way, qs, t, piece] = part[ps, t, piece].astype(jnp.bfloat16)
                                return c

                            lax.fori_loop(0, rows // 32, rows_of, 0)

                        @pl.when(k >= RECV_SLOTS)
                        def _():
                            pl.semaphore_wait(sum_free.at[way, t], 1)

                        sum_copy(k, way, t).start()

                    @pl.when((hops > 0) & (t == rank))
                    def _():
                        def rows_of(j, c):
                            piece = pl.ds(pl.multiple_of(j * 32, 32), 32)
                            part[ps, t, piece] += inc[way, es, t, piece].astype(jnp.float32)
                            return c

                        lax.fori_loop(0, rows // 32, rows_of, 0)

                    @pl.when((hops > 0) & (ahead | (t == rank)) & (k + RECV_SLOTS < n))
                    def _():
                        pl.semaphore_signal(
                            sum_free.at[way, t], inc=1, device_id=(source, ten),
                            device_id_type=MESH,
                        )

                    return carry

                lax.fori_loop(0, ranks, one_target, 0)

        f = i - 2 - last - EXTRA

        @pl.when((f >= 0) & (f < n))
        def _():
            ps = lax.rem(f, part_slots)
            s = lax.rem(f, 2)
            for copy in opts(f):
                copy.wait()

            @pl.when(f + 1 < n)
            def _():
                for copy in opts(f + 1):
                    copy.start()

            @pl.when(f >= 2)
            def _():
                for copy in results(f):
                    copy.wait()
                srv_local(f).wait()
                for d in range(1, n_ten):
                    srv_copy(f, d).wait_send()

            def rows_of(j, c):
                piece = pl.ds(pl.multiple_of(j * 32, 32), 32)
                grad = part[ps, rank, piece]
                m = 0.9 * opt_in[s, 1, piece] + 0.1 * grad
                v = 0.95 * opt_in[s, 2, piece] + 0.05 * grad * grad
                old = opt_in[s, 0, piece]
                new = old - 0.01 * ((m * FIRST) / (jnp.sqrt(v * SECOND) + 1e-08) + 0.1 * old)
                opt_out[s, 0, piece] = new
                opt_out[s, 1, piece] = m
                opt_out[s, 2, piece] = v
                return c

            lax.fori_loop(0, rows // 32, rows_of, 0)
            block = rows // n_ten
            for t in range(n_ten):
                served[s, t] = opt_out[s, 0, t * block : (t + 1) * block].astype(jnp.bfloat16)
            for d in range(1, n_ten):
                srv_copy(f, d).start()
            srv_local(f).start()
            for copy in results(f):
                copy.start()

        return carry

    lax.fori_loop(0, n + 2 + last + EXTRA, step, 0)

    for k in range(max(n - 2, 0), n):
        for copy in results(k):
            copy.wait()
        srv_local(k).wait()
        for d in range(1, n_ten):
            srv_copy(k, d).wait_send()
        for way in (0, 1):
            def drain(t, carry, way=way, k=k):
                @pl.when((t > rank) if way == 0 else (t < rank))
                def _():
                    sum_copy(k, way, t).wait_send()

                return carry

            lax.fori_loop(0, ranks, drain, 0)
    for d in range(1, n_ten):
        origin = lax.rem(ten + n_ten - d, n_ten)
        area = serving.at[
            :, pl.ds(pl.multiple_of(origin * hidden_cols, hidden_cols), hidden_cols)
        ]
        remote(area, area, srv_send.at[d - 1, 0], srv_recv.at[d - 1], me, origin).wait_recv()


def on_device(n_dp, n_ten, gate_pre, up_pre, out_grad, master, moment_one, moment_two):
    tokens, hidden_cols = gate_pre.shape
    rows = master.shape[0]
    width = 256 if hidden_cols % 256 == 0 else 128
    ranks = n_dp // GROUP
    per = ranks // n_ten
    cot = out_grad.T.reshape(per, GROUP, rows, tokens)
    part_slots = ranks + EXTRA
    f32, bf16 = jnp.float32, jnp.bfloat16
    DMA, REG = pltpu.SemaphoreType.DMA, pltpu.SemaphoreType.REGULAR
    scratch = [
        pltpu.VMEM((ranks, rows, GROUP * tokens), bf16),
        pltpu.VMEM((2, tokens, width), bf16),
        pltpu.VMEM((2, tokens, width), bf16),
        pltpu.VMEM((HID_SLOTS, GROUP * tokens, width), bf16),
        pltpu.VMEM((part_slots, ranks, rows, width), f32),
        pltpu.VMEM((2, RECV_SLOTS, ranks, rows, width), bf16),
        pltpu.VMEM((2, 2, ranks, rows, width), bf16),
        pltpu.VMEM((2, 3, rows, width), f32),
        pltpu.VMEM((2, 3, rows, width), f32),
        pltpu.VMEM((2, n_ten, rows // n_ten, width), bf16),
        DMA((GROUP - 1,)),
        DMA((GROUP - 1,)),
        DMA((n_ten - 1, GROUP)),
        DMA((n_ten - 1, GROUP)),
        DMA,
        DMA((2, 2)),
        DMA((3, HID_SLOTS)),
        DMA((3, HID_SLOTS)),
        REG((2,)),
        DMA((2, 2, ranks)),
        DMA((2, RECV_SLOTS, ranks)),
        REG((2, ranks)),
        DMA((3, 2)),
        DMA((3, 2)),
        DMA((n_ten - 1, 2)),
        DMA((n_ten - 1,)),
        DMA((2,)),
    ]
    whole = jax.ShapeDtypeStruct((rows, hidden_cols), f32)
    return pl.pallas_call(
        functools.partial(kernel, n_dp, n_ten, width),
        out_shape=(
            whole,
            whole,
            whole,
            jax.ShapeDtypeStruct((rows // n_ten, n_ten * hidden_cols), bf16),
        ),
        in_specs=[pl.BlockSpec(memory_space=pl.ANY)] * 6,
        out_specs=[pl.BlockSpec(memory_space=pl.ANY)] * 4,
        scratch_shapes=scratch,
        compiler_params=pltpu.CompilerParams(
            collective_id=0, has_side_effects=True, vmem_limit_bytes=56 * 2**20
        ),
        cost_estimate=pl.CostEstimate(
            flops=2 * rows * ranks * GROUP * tokens * hidden_cols,
            bytes_accessed=24 * rows * hidden_cols + 4 * tokens * hidden_cols,
            transcendentals=tokens * hidden_cols,
        ),
        name="grad_update",
    )(gate_pre, up_pre, cot, master, moment_one, moment_two)


def solution(mesh):
    placed = (P("dp", "tensor"),) * 6
    return jax.shard_map(
        functools.partial(on_device, mesh.shape["dp"], mesh.shape["tensor"]),
        mesh=mesh,
        in_specs=placed,
        out_specs=(
            P("dp", "tensor"),
            P("dp", "tensor"),
            P("dp", "tensor"),
            P(("dp", "tensor"), None),
        ),
        check_vma=False,
    )
```

time: 939 us -> 383 us (0.41)
  waiting for transfers between devices: 723 us -> 0 us
  Pallas kernels: 0 us -> 356 us
  local copies, waits for them, and re-layouts: 82.5 us -> 26.1 us
  blocking collectives: 52.5 us -> 0 us
  matrix products: 45.8 us -> 0 us
  other arithmetic: 19.6 us -> 0.01 us
  between operations: 14 us -> 0.67 us
    reduce_scatter x1 -> x0, waiting for transfers between devices: 649 us -> none  [on_device(): lax.psum_scatter(lax.dot_general(full_grad, hidden, contract, preferred_e...]
    pallas_call x0 -> x1, Pallas kernels: none -> 356 us  [on_device(): pl.pallas_call(functools.partial(kernel, n_dp, n_ten, width), out_shape=(...]
    all_gather x1 -> x0, waiting for transfers between devices: 72.9 us -> none  [on_device(): full_grad = lax.all_gather(out_grad, 'tensor', axis=1, tiled=True)]
    unnamed x1 -> x16, local copies, waits for them, and re-layouts: 80 us -> 21.7 us
    all_to_all x1 -> x0, blocking collectives: 52.5 us -> none  [on_device(): lax.all_to_all(master_new.astype(jnp.bfloat16), 'tensor', split_axis=0, c...]
    dot_general x1 -> x0, matrix products: 45.8 us -> none  [on_device(): lax.dot_general(full_grad, hidden, contract, preferred_element_type=jnp.f...]
    convert_element_type x1 -> x0, other arithmetic: 19.6 us -> none  [on_device(): master_new.astype(jnp.bfloat16)]
  transfers between devices with their start and end apart: 2 -> 0, of which waited for: 2 -> 0; matrix products, arithmetic and copies ran while one was open for 0% -> 0% of each run, Pallas kernels for 0% -> 0%
where the time goes in v1:
time: 383 us
  Pallas kernels  356 us (93%)
  local copies, waits for them, and re-layouts  26.1 us (7%)
    pallas_call x1, Pallas kernels, on_device(): pl.pallas_call(functools.partial(kernel, n_dp, n_ten, width), out_shape=(...  356 us
    unnamed x16, local copies, waits for them, and re-layouts  21.7 us

profile of v1, /device:TPU:0, one launch (start us, length us, event | category | flops | bytes accessed | tf_op | source)
XLA Modules:
  0.0 383.2 jit_solution(10698875243729821754)
XLA Ops:
  0.6 4.4 %copy.10 = bf16[2560,512]{1,0:T(8,128)(2,1)} copy(bf16[2560,512]{0,1:T(8,128)(2,1)} %bitcast.6) | data formatting | bytes 5242880 | tf_op jit(solution)/shard_map/transpose | solution.py:418
  5.0 356.4 %grad_update.1 = (f32[320,6656]{1,0:T(8,128)}, f32[320,6656]{1,0:T(8,128)}, f32[320,6656]{1,0:T(8,128)}, bf16[160,13312]{1,0:T(8,128)(2,1)}) custom-call(bf16[512,6656]{1,0:T(8,128)(2,1)} %gate.1, bf16[512,6656]{1,0:T(8,128)(2,1)} %up.1, bf16[2,4,320,512]{3,2,1,0:T(8,128)(2,1)} %bitcast.7, f32[320,6656]{1,0:T(8,128)} %master.1, f32[320,6656]{1,0:T(8,128)} %one.1, ...), custom_call_target="tpu_custom_call" | custom-call | flops 34896609280 | bytes 64749568 | tf_op jit(solution)/shard_map/grad_update/pallas_call | solution.py:452
  361.5 0.0 copy-start
  361.5 0.0 slice-start
  361.5 0.0 slice-start.1
  361.5 8.5 %copy.15 = f32[320,6656]{1,0:T(8,128)} copy(f32[320,6656]{1,0:T(8,128)} %get-tuple-element.8) | data formatting | bytes 17039360
  370.0 0.0 copy-done
  370.0 0.0 slice-start.2
  370.0 0.0 slice-start.3
  370.0 4.3 %copy.16 = f32[320,6656]{1,0:T(8,128)} copy(f32[320,6656]{1,0:T(8,128)S(1)} %copy-done) | data formatting | bytes 17039360
  374.3 0.0 slice-done
  374.3 1.6 slice-done.1
  375.9 0.0 slice-done.2
  375.9 0.0 slice-start.4
  375.9 4.3 %copy.17 = f32[320,6656]{1,0:T(8,128)} copy(f32[320,6656]{1,0:T(8,128)S(1)} %bitcast.3) | data formatting | bytes 17039360
  380.2 0.0 slice-done.3
  380.2 0.9 slice-done.4
  381.1 2.0 copy.18
  (2 shorter events, 0.0 us)
Async XLA Ops:
  361.5 8.5 %copy-start = (f32[320,6656]{1,0:T(8,128)S(1)}, f32[320,6656]{1,0:T(8,128)}, u32[]{:S(2)}) copy-start(f32[320,6656]{1,0:T(8,128)} %get-tuple-element.9) | copy-start | bytes 25559044
  361.5 12.8 %slice-start = ((s8[8519680]{0:T(1024)(128)(4,1)}), s8[4194304]{0:T(1024)(128)(4,1)S(1)}, s32[]{:S(2)}) async-start(s8[8519680]{0:T(1024)(128)(4,1)} %bitcast.2), calls=%async_computation | async-start | bytes 8388608
  361.5 14.4 %slice-start.1 = ((s8[8519680]{0:T(1024)(128)(4,1)}), s8[4194304]{0:T(1024)(128)(4,1)S(1)}, s32[]{:S(2)}) async-start(s8[8519680]{0:T(1024)(128)(4,1)} %bitcast.2), calls=%async_computation.1 | async-start | bytes 8388608
  370.0 5.9 %slice-start.2 = ((s8[8519680]{0:T(1024)(128)(4,1)}), s8[131072]{0:T(1024)(128)(4,1)S(1)}, s32[]{:S(2)}) async-start(s8[8519680]{0:T(1024)(128)(4,1)} %bitcast.2), calls=%async_computation.2 | async-start | bytes 262144
  370.0 10.2 %slice-start.3 = ((s8[4259840]{0:T(1024)(128)(4,1)}), s8[65536]{0:T(1024)(128)(4,1)S(1)}, s32[]{:S(2)}) async-start(s8[4259840]{0:T(1024)(128)(4,1)} %bitcast.4), calls=%async_computation.3 | async-start | bytes 131072
  375.9 5.3 %slice-start.4 = ((s8[4259840]{0:T(1024)(128)(4,1)}), s8[4194304]{0:T(1024)(128)(4,1)S(1)}, s32[]{:S(2)}) async-start(s8[4259840]{0:T(1024)(128)(4,1)} %bitcast.4), calls=%async_computation.4 | async-start | bytes 8388608

commit v2 on v1

--- a/solution.py
+++ b/solution.py
@@ -9,7 +9,8 @@
 
 MESH = pl.DeviceIdType.MESH
 GROUP = 4
-HID_SLOTS = 4
+LATE = 6
+HID_SLOTS = 4 + LATE
 RECV_SLOTS = 3
 EXTRA = 1
 FIRST = 1.0 / (1.0 - 0.9**20)
@@ -88,6 +89,9 @@
         pl.semaphore_signal(barrier, inc=1, device_id=(other, ten), device_id_type=MESH)
     pl.semaphore_wait(barrier, len(peers) + len(partners) + 2)
 
+    def lag(t):
+        return jnp.where(lax.div(t, per) == ten, 0, LATE)
+
     def cols(k):
         return pl.ds(pl.multiple_of(k * width, width), width)
 
@@ -236,11 +240,14 @@
         @pl.when(c == 0)
         def _():
             own_cot().wait()
+            for d in range(1, GROUP):
+                cot_out(d).wait_send()
+
+        @pl.when(c == LATE)
+        def _():
             for d in range(GROUP):
                 for e in range(1, n_ten):
                     cot_fwd(d, e).wait()
-            for d in range(1, GROUP):
-                cot_out(d).wait_send()
 
         @pl.when((c >= 0) & (c < n))
         def _():
@@ -248,40 +255,46 @@
             hid_copy(c, 0).wait_recv()
             hid_copy(c, 2).wait_recv()
 
-            def product(t, carry):
-                part[lax.rem(c, part_slots), t] = jnp.dot(
-                    cot_all[t], hid[s], preferred_element_type=jnp.float32
-                )
-                return carry
-
-            lax.fori_loop(0, ranks, product, 0)
             for which in range(3):
                 hid_copy(c, which).wait_send()
 
-            @pl.when(c + HID_SLOTS < n)
+        def product(t, carry):
+            k = c - lag(t)
+
+            @pl.when((k >= 0) & (k < n))
             def _():
-                pl.semaphore_signal(
-                    hid_free.at[0], inc=1, device_id=(sib, ten), device_id_type=MESH
+                part[lax.rem(k, part_slots), t] = jnp.dot(
+                    cot_all[t], hid[lax.rem(k, HID_SLOTS)], preferred_element_type=jnp.float32
                 )
-                pl.semaphore_signal(
-                    hid_free.at[1], inc=1, device_id=(far, ten), device_id_type=MESH
-                )
+
+            return carry
+
+        lax.fori_loop(0, ranks, product, 0)
+
+        @pl.when((c >= LATE) & (c - LATE + HID_SLOTS < n))
+        def _():
+            pl.semaphore_signal(
+                hid_free.at[0], inc=1, device_id=(sib, ten), device_id_type=MESH
+            )
+            pl.semaphore_signal(
+                hid_free.at[1], inc=1, device_id=(far, ten), device_id_type=MESH
+            )
 
         for way in (0, 1):
             hops = rank if way == 0 else last - rank
-            k = i - 2 - hops
             source = below if way == 0 else above
 
-            @pl.when((k >= 0) & (k < n))
-            def _(way=way, hops=hops, k=k, source=source):
-                ps = lax.rem(k, part_slots)
-                es = lax.rem(k, RECV_SLOTS)
-                qs = lax.rem(k, 2)
-
-                def one_target(t, carry):
-                    ahead = (t > rank) if way == 0 else (t < rank)
-
-                    @pl.when((hops > 0) & (ahead | (t == rank)))
+            def one_target(t, carry, way=way, hops=hops, source=source):
+                k = i - 2 - hops - lag(t)
+                ahead = (t > rank) if way == 0 else (t < rank)
+
+                @pl.when((k >= 0) & (k < n) & (ahead | ((t == rank) & (hops > 0))))
+                def _():
+                    ps = lax.rem(k, part_slots)
+                    es = lax.rem(k, RECV_SLOTS)
+                    qs = lax.rem(k, 2)
+
+                    @pl.when(hops > 0)
                     def _():
                         sum_copy(k, way, t).wait_recv()
 
@@ -318,7 +331,7 @@
 
                         sum_copy(k, way, t).start()
 
-                    @pl.when((hops > 0) & (t == rank))
+                    @pl.when(t == rank)
                     def _():
                         def rows_of(j, c):
                             piece = pl.ds(pl.multiple_of(j * 32, 32), 32)
@@ -327,18 +340,18 @@
 
                         lax.fori_loop(0, rows // 32, rows_of, 0)
 
-                    @pl.when((hops > 0) & (ahead | (t == rank)) & (k + RECV_SLOTS < n))
+                    @pl.when((hops > 0) & (k + RECV_SLOTS < n))
                     def _():
                         pl.semaphore_signal(
                             sum_free.at[way, t], inc=1, device_id=(source, ten),
                             device_id_type=MESH,
                         )
 
-                    return carry
-
-                lax.fori_loop(0, ranks, one_target, 0)
-
-        f = i - 2 - last - EXTRA
+                return carry
+
+            lax.fori_loop(0, ranks, one_target, 0)
+
+        f = i - 2 - last - EXTRA - lag(rank)
 
         @pl.when((f >= 0) & (f < n))
         def _():
@@ -384,7 +397,7 @@
 
         return carry
 
-    lax.fori_loop(0, n + 2 + last + EXTRA, step, 0)
+    lax.fori_loop(0, n + 2 + last + EXTRA + LATE, step, 0)
 
     for k in range(max(n - 2, 0), n):
         for copy in results(k):

time: 383 us -> 387 us (1.010)
  Pallas kernels: 356 us -> 360 us
where the time goes in v2:
time: 387 us; the launch traced here: 386 us
  Pallas kernels  360 us (93%)
  local copies, waits for them, and re-layouts  26.1 us (7%)
    pallas_call x1, Pallas kernels, on_device(): pl.pallas_call(functools.partial(kernel, n_dp, n_ten, width), out_shape=(...  360 us
    unnamed x16, local copies, waits for them, and re-layouts  21.7 us

profile of v2, /device:TPU:0, one launch (start us, length us, event | category | flops | bytes accessed | tf_op | source)
XLA Modules:
  0.0 386.4 jit_solution(6433800281805147462)
XLA Ops:
  0.6 4.4 %copy.10 = bf16[2560,512]{1,0:T(8,128)(2,1)} copy(bf16[2560,512]{0,1:T(8,128)(2,1)} %bitcast.6) | data formatting | bytes 5242880 | tf_op jit(solution)/shard_map/transpose | solution.py:431
  5.0 359.7 %grad_update.1 = (f32[320,6656]{1,0:T(8,128)}, f32[320,6656]{1,0:T(8,128)}, f32[320,6656]{1,0:T(8,128)}, bf16[160,13312]{1,0:T(8,128)(2,1)}) custom-call(bf16[512,6656]{1,0:T(8,128)(2,1)} %gate.1, bf16[512,6656]{1,0:T(8,128)(2,1)} %up.1, bf16[2,4,320,512]{3,2,1,0:T(8,128)(2,1)} %bitcast.7, f32[320,6656]{1,0:T(8,128)} %master.1, f32[320,6656]{1,0:T(8,128)} %one.1, ...), custom_call_target="tpu_custom_call" | custom-call | flops 34896609280 | bytes 64749568 | tf_op jit(solution)/shard_map/grad_update/pallas_call | solution.py:465
  364.7 0.0 copy-start
  364.7 0.0 slice-start
  364.7 0.0 slice-start.1
  364.7 8.5 %copy.15 = f32[320,6656]{1,0:T(8,128)} copy(f32[320,6656]{1,0:T(8,128)} %get-tuple-element.8) | data formatting | bytes 17039360
  373.2 0.0 copy-done
  373.2 0.0 slice-start.2
  373.2 0.0 slice-start.3
  373.2 4.3 %copy.16 = f32[320,6656]{1,0:T(8,128)} copy(f32[320,6656]{1,0:T(8,128)S(1)} %copy-done) | data formatting | bytes 17039360
  377.5 0.0 slice-done
  377.5 1.6 slice-done.1
  379.1 0.0 slice-done.2
  379.1 0.0 slice-start.4
  379.1 4.3 %copy.17 = f32[320,6656]{1,0:T(8,128)} copy(f32[320,6656]{1,0:T(8,128)S(1)} %bitcast.3) | data formatting | bytes 17039360
  383.4 0.0 slice-done.3
  383.4 0.9 slice-done.4
  384.4 2.0 copy.18
  (2 shorter events, 0.0 us)
Async XLA Ops:
  364.7 8.5 %copy-start = (f32[320,6656]{1,0:T(8,128)S(1)}, f32[320,6656]{1,0:T(8,128)}, u32[]{:S(2)}) copy-start(f32[320,6656]{1,0:T(8,128)} %get-tuple-element.9) | copy-start | bytes 25559044
  364.7 12.8 %slice-start = ((s8[8519680]{0:T(1024)(128)(4,1)}), s8[4194304]{0:T(1024)(128)(4,1)S(1)}, s32[]{:S(2)}) async-start(s8[8519680]{0:T(1024)(128)(4,1)} %bitcast.2), calls=%async_computation | async-start | bytes 8388608
  364.7 14.4 %slice-start.1 = ((s8[8519680]{0:T(1024)(128)(4,1)}), s8[4194304]{0:T(1024)(128)(4,1)S(1)}, s32[]{:S(2)}) async-start(s8[8519680]{0:T(1024)(128)(4,1)} %bitcast.2), calls=%async_computation.1 | async-start | bytes 8388608
  373.2 5.9 %slice-start.2 = ((s8[8519680]{0:T(1024)(128)(4,1)}), s8[131072]{0:T(1024)(128)(4,1)S(1)}, s32[]{:S(2)}) async-start(s8[8519680]{0:T(1024)(128)(4,1)} %bitcast.2), calls=%async_computation.2 | async-start | bytes 262144
  373.2 10.2 %slice-start.3 = ((s8[4259840]{0:T(1024)(128)(4,1)}), s8[65536]{0:T(1024)(128)(4,1)S(1)}, s32[]{:S(2)}) async-start(s8[4259840]{0:T(1024)(128)(4,1)} %bitcast.4), calls=%async_computation.3 | async-start | bytes 131072
  379.1 5.3 %slice-start.4 = ((s8[4259840]{0:T(1024)(128)(4,1)}), s8[4194304]{0:T(1024)(128)(4,1)S(1)}, s32[]{:S(2)}) async-start(s8[4259840]{0:T(1024)(128)(4,1)} %bitcast.4), calls=%async_computation.4 | async-start | bytes 8388608

commit v3 on v2

--- a/solution.py
+++ b/solution.py
@@ -9,7 +9,7 @@
 
 MESH = pl.DeviceIdType.MESH
 GROUP = 4
-LATE = 6
+LATE = 4
 HID_SLOTS = 4 + LATE
 RECV_SLOTS = 3
 EXTRA = 1
@@ -92,6 +92,11 @@
     def lag(t):
         return jnp.where(lax.div(t, per) == ten, 0, LATE)
 
+    big, small = rows // 2, rows // 5
+
+    def here(t, j, size):
+        return pl.ds(pl.multiple_of(t * rows + j * size, 16), size)
+
     def cols(k):
         return pl.ds(pl.multiple_of(k * width, width), width)
 
@@ -109,24 +114,25 @@
         )
 
     def cot_here(who):
-        return cot_all.at[pl.ds(ten * per, per), :, toks(who)]
+        half = per * rows
+        return cot_all.at[pl.ds(pl.multiple_of(ten * half, half), half), toks(who)]
 
     def cot_out(d):
         to = lax.rem(g + d, GROUP)
         return remote(
-            cot.at[:, to], cot_here(g), cot_send.at[d - 1], cot_recv.at[d - 1],
+            cot.at[to], cot_here(g), cot_send.at[d - 1], cot_recv.at[d - 1],
             rank * GROUP + to, ten,
         )
 
     def cot_fwd(d, e):
-        src = cot.at[:, g] if d == 0 else cot_here(lax.rem(g + GROUP - d, GROUP))
+        src = cot.at[g] if d == 0 else cot_here(lax.rem(g + GROUP - d, GROUP))
         return remote(
             src, cot_here(lax.rem(g + GROUP - d, GROUP)),
             fwd_send.at[e - 1, d], fwd_recv.at[e - 1, d], me, lax.rem(ten + e, n_ten),
         )
 
     def own_cot():
-        return pltpu.make_async_copy(cot.at[:, g], cot_here(g), own_sem)
+        return pltpu.make_async_copy(cot.at[g], cot_here(g), own_sem)
 
     def acts(k):
         s = lax.rem(k, 2)
@@ -203,15 +209,15 @@
                     copy.start()
 
             def rows_of(j, c):
-                piece = pl.ds(pl.multiple_of(j * 64, 64), 64)
+                piece = pl.ds(pl.multiple_of(j * 128, 128), 128)
                 v = gates[q, piece].astype(jnp.float32)
                 u = ups[q, piece].astype(jnp.float32)
                 value = (0.5 * v) * (1.0 + jnp.tanh(0.5 * v)) * u
-                place = pl.ds(pl.multiple_of(g * tokens + j * 64, 64), 64)
+                place = pl.ds(pl.multiple_of(g * tokens + j * 128, 128), 128)
                 hid[s, place] = value.astype(jnp.bfloat16)
                 return c
 
-            lax.fori_loop(0, tokens // 64, rows_of, 0)
+            lax.fori_loop(0, tokens // 128, rows_of, 0)
 
             @pl.when(i >= HID_SLOTS)
             def _():
@@ -258,18 +264,20 @@
             for which in range(3):
                 hid_copy(c, which).wait_send()
 
-        def product(t, carry):
-            k = c - lag(t)
+        def product(j, carry):
+            k = c - jnp.where(j == ten, 0, LATE)
 
             @pl.when((k >= 0) & (k < n))
             def _():
-                part[lax.rem(k, part_slots), t] = jnp.dot(
-                    cot_all[t], hid[lax.rem(k, HID_SLOTS)], preferred_element_type=jnp.float32
+                half = per * rows
+                place = pl.ds(pl.multiple_of(j * half, half), half)
+                part[lax.rem(k, part_slots), place] = jnp.dot(
+                    cot_all[place], hid[lax.rem(k, HID_SLOTS)], preferred_element_type=jnp.float32
                 )
 
             return carry
 
-        lax.fori_loop(0, ranks, product, 0)
+        lax.fori_loop(0, n_ten, product, 0)
 
         @pl.when((c >= LATE) & (c - LATE + HID_SLOTS < n))
         def _():
@@ -307,23 +315,23 @@
                         @pl.when(hops > 0)
                         def _():
                             def rows_of(j, c):
-                                piece = pl.ds(pl.multiple_of(j * 32, 32), 32)
-                                value = part[ps, t, piece] + inc[way, es, t, piece].astype(
+                                piece = pl.ds(pl.multiple_of(j * big, big), big)
+                                value = part[ps, here(t, j, big)] + inc[way, es, t, piece].astype(
                                     jnp.float32
                                 )
                                 outg[way, qs, t, piece] = value.astype(jnp.bfloat16)
                                 return c
 
-                            lax.fori_loop(0, rows // 32, rows_of, 0)
+                            lax.fori_loop(0, rows // big, rows_of, 0)
 
                         @pl.when(hops == 0)
                         def _():
                             def rows_of(j, c):
-                                piece = pl.ds(pl.multiple_of(j * 32, 32), 32)
-                                outg[way, qs, t, piece] = part[ps, t, piece].astype(jnp.bfloat16)
+                                piece = pl.ds(pl.multiple_of(j * big, big), big)
+                                outg[way, qs, t, piece] = part[ps, here(t, j, big)].astype(jnp.bfloat16)
                                 return c
 
-                            lax.fori_loop(0, rows // 32, rows_of, 0)
+                            lax.fori_loop(0, rows // big, rows_of, 0)
 
                         @pl.when(k >= RECV_SLOTS)
                         def _():
@@ -334,11 +342,11 @@
                     @pl.when(t == rank)
                     def _():
                         def rows_of(j, c):
-                            piece = pl.ds(pl.multiple_of(j * 32, 32), 32)
-                            part[ps, t, piece] += inc[way, es, t, piece].astype(jnp.float32)
+                            piece = pl.ds(pl.multiple_of(j * big, big), big)
+                            part[ps, here(t, j, big)] += inc[way, es, t, piece].astype(jnp.float32)
                             return c
 
-                        lax.fori_loop(0, rows // 32, rows_of, 0)
+                        lax.fori_loop(0, rows // big, rows_of, 0)
 
                     @pl.when((hops > 0) & (k + RECV_SLOTS < n))
                     def _():
@@ -374,8 +382,8 @@
                     srv_copy(f, d).wait_send()
 
             def rows_of(j, c):
-                piece = pl.ds(pl.multiple_of(j * 32, 32), 32)
-                grad = part[ps, rank, piece]
+                piece = pl.ds(pl.multiple_of(j * small, small), small)
+                grad = part[ps, here(rank, j, small)]
                 m = 0.9 * opt_in[s, 1, piece] + 0.1 * grad
                 v = 0.95 * opt_in[s, 2, piece] + 0.05 * grad * grad
                 old = opt_in[s, 0, piece]
@@ -385,7 +393,7 @@
                 opt_out[s, 2, piece] = v
                 return c
 
-            lax.fori_loop(0, rows // 32, rows_of, 0)
+            lax.fori_loop(0, rows // small, rows_of, 0)
             block = rows // n_ten
             for t in range(n_ten):
                 served[s, t] = opt_out[s, 0, t * block : (t + 1) * block].astype(jnp.bfloat16)
@@ -428,16 +436,17 @@
     width = 256 if hidden_cols % 256 == 0 else 128
     ranks = n_dp // GROUP
     per = ranks // n_ten
-    cot = out_grad.T.reshape(per, GROUP, rows, tokens)
+    cot = out_grad.T.reshape(per, GROUP, rows, tokens).swapaxes(0, 1)
+    cot = cot.reshape(GROUP, per * rows, tokens)
     part_slots = ranks + EXTRA
     f32, bf16 = jnp.float32, jnp.bfloat16
     DMA, REG = pltpu.SemaphoreType.DMA, pltpu.SemaphoreType.REGULAR
     scratch = [
-        pltpu.VMEM((ranks, rows, GROUP * tokens), bf16),
+        pltpu.VMEM((ranks * rows, GROUP * tokens), bf16),
         pltpu.VMEM((2, tokens, width), bf16),
         pltpu.VMEM((2, tokens, width), bf16),
         pltpu.VMEM((HID_SLOTS, GROUP * tokens, width), bf16),
-        pltpu.VMEM((part_slots, ranks, rows, width), f32),
+        pltpu.VMEM((part_slots, ranks * rows, width), f32),
         pltpu.VMEM((2, RECV_SLOTS, ranks, rows, width), bf16),
         pltpu.VMEM((2, 2, ranks, rows, width), bf16),
         pltpu.VMEM((2, 3, rows, width), f32),

time: 387 us -> 379 us (0.979)
  Pallas kernels: 360 us -> 352 us
    pallas_call x1, Pallas kernels: 360 us -> 352 us  [on_device(): pl.pallas_call(functools.partial(kernel, n_dp, n_ten, width), out_shape=(...]
    unnamed x16 -> x17, local copies, waits for them, and re-layouts: 21.7 us -> 24.7 us
where the time goes in v3:
time: 379 us
  Pallas kernels  352 us (93%)
  local copies, waits for them, and re-layouts  26.4 us (7%)
    pallas_call x1, Pallas kernels, on_device(): pl.pallas_call(functools.partial(kernel, n_dp, n_ten, width), out_shape=(...  352 us
    unnamed x17, local copies, waits for them, and re-layouts  24.7 us

profile of v3, /device:TPU:0, one launch (start us, length us, event | category | flops | bytes accessed | tf_op | source)
XLA Modules:
  0.0 379.0 jit_solution(7244643413257207099)
XLA Ops:
  0.6 3.0 copy.11
  3.6 1.8 copy.12
  5.4 351.8 %grad_update.1 = (f32[320,6656]{1,0:T(8,128)}, f32[320,6656]{1,0:T(8,128)}, f32[320,6656]{1,0:T(8,128)}, bf16[160,13312]{1,0:T(8,128)(2,1)}) custom-call(bf16[512,6656]{1,0:T(8,128)(2,1)} %gate.1, bf16[512,6656]{1,0:T(8,128)(2,1)} %up.1, bf16[4,640,512]{2,1,0:T(8,128)(2,1)} %bitcast.11, f32[320,6656]{1,0:T(8,128)} %master.1, f32[320,6656]{1,0:T(8,128)} %one.1, ...), custom_call_target="tpu_custom_call" | custom-call | flops 34896609280 | bytes 64749568 | tf_op jit(solution)/shard_map/grad_update/pallas_call | solution.py:474
  357.3 0.0 copy-start
  357.3 0.0 slice-start
  357.3 0.0 slice-start.1
  357.3 8.5 %copy.17 = f32[320,6656]{1,0:T(8,128)} copy(f32[320,6656]{1,0:T(8,128)} %get-tuple-element.8) | data formatting | bytes 17039360
  365.8 0.0 copy-done
  365.8 0.0 slice-start.2
  365.8 0.0 slice-start.3
  365.8 4.3 %copy.18 = f32[320,6656]{1,0:T(8,128)} copy(f32[320,6656]{1,0:T(8,128)S(1)} %copy-done) | data formatting | bytes 17039360
  370.1 0.0 slice-done
  370.1 1.6 slice-done.1
  371.7 0.0 slice-done.2
  371.7 0.0 slice-start.4
  371.7 4.3 %copy.19 = f32[320,6656]{1,0:T(8,128)} copy(f32[320,6656]{1,0:T(8,128)S(1)} %bitcast.8) | data formatting | bytes 17039360
  376.0 0.0 slice-done.3
  376.0 0.9 slice-done.4
  376.9 2.0 copy.20
  (2 shorter events, 0.0 us)
Async XLA Ops:
  357.3 8.5 %copy-start = (f32[320,6656]{1,0:T(8,128)S(1)}, f32[320,6656]{1,0:T(8,128)}, u32[]{:S(2)}) copy-start(f32[320,6656]{1,0:T(8,128)} %get-tuple-element.9) | copy-start | bytes 25559044
  357.3 12.8 %slice-start = ((s8[8519680]{0:T(1024)(128)(4,1)}), s8[4194304]{0:T(1024)(128)(4,1)S(1)}, s32[]{:S(2)}) async-start(s8[8519680]{0:T(1024)(128)(4,1)} %bitcast.7), calls=%async_computation | async-start | bytes 8388608
  357.3 14.4 %slice-start.1 = ((s8[8519680]{0:T(1024)(128)(4,1)}), s8[4194304]{0:T(1024)(128)(4,1)S(1)}, s32[]{:S(2)}) async-start(s8[8519680]{0:T(1024)(128)(4,1)} %bitcast.7), calls=%async_computation.1 | async-start | bytes 8388608
  365.8 5.9 %slice-start.2 = ((s8[8519680]{0:T(1024)(128)(4,1)}), s8[131072]{0:T(1024)(128)(4,1)S(1)}, s32[]{:S(2)}) async-start(s8[8519680]{0:T(1024)(128)(4,1)} %bitcast.7), calls=%async_computation.2 | async-start | bytes 262144
  365.8 10.2 %slice-start.3 = ((s8[4259840]{0:T(1024)(128)(4,1)}), s8[65536]{0:T(1024)(128)(4,1)S(1)}, s32[]{:S(2)}) async-start(s8[4259840]{0:T(1024)(128)(4,1)} %bitcast.9), calls=%async_computation.3 | async-start | bytes 131072
  371.7 5.3 %slice-start.4 = ((s8[4259840]{0:T(1024)(128)(4,1)}), s8[4194304]{0:T(1024)(128)(4,1)S(1)}, s32[]{:S(2)}) async-start(s8[4259840]{0:T(1024)(128)(4,1)} %bitcast.9), calls=%async_computation.4 | async-start | bytes 8388608

commit v4 on v3

--- a/solution.py
+++ b/solution.py
@@ -11,8 +11,10 @@
 GROUP = 4
 LATE = 4
 HID_SLOTS = 4 + LATE
-RECV_SLOTS = 3
-EXTRA = 1
+RECV_SLOTS = 5
+SEND_SLOTS = 3
+HOP = 2
+EXTRA = 0
 FIRST = 1.0 / (1.0 - 0.9**20)
 SECOND = 1.0 / (1.0 - 0.95**20)
 
@@ -162,7 +164,7 @@
         return remote(block, block, hid_send.at[which, s], hid_recv.at[which, s], to, ten)
 
     def sum_copy(k, way, t):
-        s = lax.rem(k, 2)
+        s = lax.rem(k, SEND_SLOTS)
         e = lax.rem(k, RECV_SLOTS)
         return remote(
             outg.at[way, s, t], inc.at[way, e, t], sum_send.at[way, s, t],
@@ -293,14 +295,14 @@
             source = below if way == 0 else above
 
             def one_target(t, carry, way=way, hops=hops, source=source):
-                k = i - 2 - hops - lag(t)
+                k = i - 2 - HOP * hops - lag(t)
                 ahead = (t > rank) if way == 0 else (t < rank)
 
                 @pl.when((k >= 0) & (k < n) & (ahead | ((t == rank) & (hops > 0))))
                 def _():
                     ps = lax.rem(k, part_slots)
                     es = lax.rem(k, RECV_SLOTS)
-                    qs = lax.rem(k, 2)
+                    qs = lax.rem(k, SEND_SLOTS)
 
                     @pl.when(hops > 0)
                     def _():
@@ -308,7 +310,7 @@
 
                     @pl.when(ahead)
                     def _():
-                        @pl.when(k >= 2)
+                        @pl.when(k >= SEND_SLOTS)
                         def _():
                             sum_copy(k, way, t).wait_send()
 
@@ -359,7 +361,7 @@
 
             lax.fori_loop(0, ranks, one_target, 0)
 
-        f = i - 2 - last - EXTRA - lag(rank)
+        f = i - 2 - HOP * last - EXTRA - lag(rank)
 
         @pl.when((f >= 0) & (f < n))
         def _():
@@ -405,7 +407,7 @@
 
         return carry
 
-    lax.fori_loop(0, n + 2 + last + EXTRA + LATE, step, 0)
+    lax.fori_loop(0, n + 2 + HOP * last + EXTRA + LATE, step, 0)
 
     for k in range(max(n - 2, 0), n):
         for copy in results(k):
@@ -413,6 +415,7 @@
         srv_local(k).wait()
         for d in range(1, n_ten):
             srv_copy(k, d).wait_send()
+    for k in range(max(n - SEND_SLOTS, 0), n):
         for way in (0, 1):
             def drain(t, carry, way=way, k=k):
                 @pl.when((t > rank) if way == 0 else (t < rank))
@@ -438,7 +441,7 @@
     per = ranks // n_ten
     cot = out_grad.T.reshape(per, GROUP, rows, tokens).swapaxes(0, 1)
     cot = cot.reshape(GROUP, per * rows, tokens)
-    part_slots = ranks + EXTRA
+    part_slots = HOP * (ranks - 1) + 1 + EXTRA
     f32, bf16 = jnp.float32, jnp.bfloat16
     DMA, REG = pltpu.SemaphoreType.DMA, pltpu.SemaphoreType.REGULAR
     scratch = [
@@ -448,7 +451,7 @@
         pltpu.VMEM((HID_SLOTS, GROUP * tokens, width), bf16),
         pltpu.VMEM((part_slots, ranks * rows, width), f32),
         pltpu.VMEM((2, RECV_SLOTS, ranks, rows, width), bf16),
-        pltpu.VMEM((2, 2, ranks, rows, width), bf16),
+        pltpu.VMEM((2, SEND_SLOTS, ranks, rows, width), bf16),
         pltpu.VMEM((2, 3, rows, width), f32),
         pltpu.VMEM((2, 3, rows, width), f32),
         pltpu.VMEM((2, n_ten, rows // n_ten, width), bf16),
@@ -461,7 +464,7 @@
         DMA((3, HID_SLOTS)),
         DMA((3, HID_SLOTS)),
         REG((2,)),
-        DMA((2, 2, ranks)),
+        DMA((2, SEND_SLOTS, ranks)),
         DMA((2, RECV_SLOTS, ranks)),
         REG((2, ranks)),
         DMA((3, 2)),

time: 379 us -> 373 us (0.984)
  Pallas kernels: 352 us -> 346 us
    pallas_call x1, Pallas kernels: 352 us -> 346 us  [on_device(): pl.pallas_call(functools.partial(kernel, n_dp, n_ten, width), out_shape=(...]
where the time goes in v4:
time: 373 us
  Pallas kernels  346 us (93%)
  local copies, waits for them, and re-layouts  26.4 us (7%)
    pallas_call x1, Pallas kernels, on_device(): pl.pallas_call(functools.partial(kernel, n_dp, n_ten, width), out_shape=(...  346 us
    unnamed x17, local copies, waits for them, and re-layouts  24.7 us

profile of v4, /device:TPU:0, one launch (start us, length us, event | category | flops | bytes accessed | tf_op | source)
XLA Modules:
  0.0 372.9 jit_solution(2162127647948595978)
XLA Ops:
  0.6 3.0 copy.11
  3.6 1.8 copy.12
  5.4 345.7 %grad_update.1 = (f32[320,6656]{1,0:T(8,128)}, f32[320,6656]{1,0:T(8,128)}, f32[320,6656]{1,0:T(8,128)}, bf16[160,13312]{1,0:T(8,128)(2,1)}) custom-call(bf16[512,6656]{1,0:T(8,128)(2,1)} %gate.1, bf16[512,6656]{1,0:T(8,128)(2,1)} %up.1, bf16[4,640,512]{2,1,0:T(8,128)(2,1)} %bitcast.11, f32[320,6656]{1,0:T(8,128)} %master.1, f32[320,6656]{1,0:T(8,128)} %one.1, ...), custom_call_target="tpu_custom_call" | custom-call | flops 34896609280 | bytes 64749568 | tf_op jit(solution)/shard_map/grad_update/pallas_call | solution.py:477
  351.2 0.0 copy-start
  351.2 0.0 slice-start
  351.2 0.0 slice-start.1
  351.2 8.5 %copy.17 = f32[320,6656]{1,0:T(8,128)} copy(f32[320,6656]{1,0:T(8,128)} %get-tuple-element.8) | data formatting | bytes 17039360
  359.7 0.0 copy-done
  359.7 0.0 slice-start.2
  359.7 0.0 slice-start.3
  359.7 4.3 %copy.18 = f32[320,6656]{1,0:T(8,128)} copy(f32[320,6656]{1,0:T(8,128)S(1)} %copy-done) | data formatting | bytes 17039360
  364.0 0.0 slice-done
  364.0 1.6 slice-done.1
  365.5 0.0 slice-done.2
  365.6 0.0 slice-start.4
  365.6 4.3 %copy.19 = f32[320,6656]{1,0:T(8,128)} copy(f32[320,6656]{1,0:T(8,128)S(1)} %bitcast.8) | data formatting | bytes 17039360
  369.9 0.0 slice-done.3
  369.9 0.9 slice-done.4
  370.8 2.0 copy.20
  (2 shorter events, 0.0 us)
Async XLA Ops:
  351.2 8.5 %copy-start = (f32[320,6656]{1,0:T(8,128)S(1)}, f32[320,6656]{1,0:T(8,128)}, u32[]{:S(2)}) copy-start(f32[320,6656]{1,0:T(8,128)} %get-tuple-element.9) | copy-start | bytes 25559044
  351.2 12.8 %slice-start = ((s8[8519680]{0:T(1024)(128)(4,1)}), s8[4194304]{0:T(1024)(128)(4,1)S(1)}, s32[]{:S(2)}) async-start(s8[8519680]{0:T(1024)(128)(4,1)} %bitcast.7), calls=%async_computation | async-start | bytes 8388608
  351.2 14.4 %slice-start.1 = ((s8[8519680]{0:T(1024)(128)(4,1)}), s8[4194304]{0:T(1024)(128)(4,1)S(1)}, s32[]{:S(2)}) async-start(s8[8519680]{0:T(1024)(128)(4,1)} %bitcast.7), calls=%async_computation.1 | async-start | bytes 8388608
  359.7 5.9 %slice-start.2 = ((s8[8519680]{0:T(1024)(128)(4,1)}), s8[131072]{0:T(1024)(128)(4,1)S(1)}, s32[]{:S(2)}) async-start(s8[8519680]{0:T(1024)(128)(4,1)} %bitcast.7), calls=%async_computation.2 | async-start | bytes 262144
  359.7 10.2 %slice-start.3 = ((s8[4259840]{0:T(1024)(128)(4,1)}), s8[65536]{0:T(1024)(128)(4,1)S(1)}, s32[]{:S(2)}) async-start(s8[4259840]{0:T(1024)(128)(4,1)} %bitcast.9), calls=%async_computation.3 | async-start | bytes 131072
  365.6 5.3 %slice-start.4 = ((s8[4259840]{0:T(1024)(128)(4,1)}), s8[4194304]{0:T(1024)(128)(4,1)S(1)}, s32[]{:S(2)}) async-start(s8[4259840]{0:T(1024)(128)(4,1)} %bitcast.9), calls=%async_computation.4 | async-start | bytes 8388608

commit v5 on v4

--- a/solution.py
+++ b/solution.py
@@ -76,7 +76,9 @@
     sib = me + 1 - 2 * lax.rem(g, 2)
     far = me + 2 - 4 * lax.div(g, 2)
     g_far = g + 2 - 4 * lax.div(g, 2)
-    peers = [rank * GROUP + lax.rem(g + d, GROUP) for d in range(1, GROUP)]
+    g_sib = g + 1 - 2 * lax.rem(g, 2)
+    near = [g, g_sib, g_far, g_far + g_sib - g]
+    peers = [rank * GROUP + who for who in near[1:]]
     partners = [lax.rem(ten + d, n_ten) for d in range(1, n_ten)]
     below = me - GROUP
     above = me + GROUP
@@ -120,16 +122,16 @@
         return cot_all.at[pl.ds(pl.multiple_of(ten * half, half), half), toks(who)]
 
     def cot_out(d):
-        to = lax.rem(g + d, GROUP)
+        to = near[d]
         return remote(
             cot.at[to], cot_here(g), cot_send.at[d - 1], cot_recv.at[d - 1],
             rank * GROUP + to, ten,
         )
 
     def cot_fwd(d, e):
-        src = cot.at[g] if d == 0 else cot_here(lax.rem(g + GROUP - d, GROUP))
+        src = cot.at[g] if d == 0 else cot_here(near[d])
         return remote(
-            src, cot_here(lax.rem(g + GROUP - d, GROUP)),
+            src, cot_here(near[d]),
             fwd_send.at[e - 1, d], fwd_recv.at[e - 1, d], me, lax.rem(ten + e, n_ten),
         )
 
@@ -294,7 +296,8 @@
             hops = rank if way == 0 else last - rank
             source = below if way == 0 else above
 
-            def one_target(t, carry, way=way, hops=hops, source=source):
+            def one_target(j, carry, way=way, hops=hops, source=source):
+                t = last - j if way == 0 else j
                 k = i - 2 - HOP * hops - lag(t)
                 ahead = (t > rank) if way == 0 else (t < rank)
 
@@ -316,9 +319,9 @@
 
                         @pl.when(hops > 0)
                         def _():
-                            def rows_of(j, c):
-                                piece = pl.ds(pl.multiple_of(j * big, big), big)
-                                value = part[ps, here(t, j, big)] + inc[way, es, t, piece].astype(
+                            def rows_of(h, c):
+                                piece = pl.ds(pl.multiple_of(h * big, big), big)
+                                value = part[ps, here(t, h, big)] + inc[way, es, t, piece].astype(
                                     jnp.float32
                                 )
                                 outg[way, qs, t, piece] = value.astype(jnp.bfloat16)
@@ -328,9 +331,9 @@
 
                         @pl.when(hops == 0)
                         def _():
-                            def rows_of(j, c):
-                                piece = pl.ds(pl.multiple_of(j * big, big), big)
-                                outg[way, qs, t, piece] = part[ps, here(t, j, big)].astype(jnp.bfloat16)
+                            def rows_of(h, c):
+                                piece = pl.ds(pl.multiple_of(h * big, big), big)
+                                outg[way, qs, t, piece] = part[ps, here(t, h, big)].astype(jnp.bfloat16)
                                 return c
 
                             lax.fori_loop(0, rows // big, rows_of, 0)
@@ -343,9 +346,9 @@
 
                     @pl.when(t == rank)
                     def _():
-                        def rows_of(j, c):
-                            piece = pl.ds(pl.multiple_of(j * big, big), big)
-                            part[ps, here(t, j, big)] += inc[way, es, t, piece].astype(jnp.float32)
+                        def rows_of(h, c):
+                            piece = pl.ds(pl.multiple_of(h * big, big), big)
+                            part[ps, here(t, h, big)] += inc[way, es, t, piece].astype(jnp.float32)
                             return c
 
                         lax.fori_loop(0, rows // big, rows_of, 0)

time: 373 us -> 373 us (level)
  no operation moved by 1% of the time
where the time goes in v5:
time: 373 us
  Pallas kernels  346 us (93%)
  local copies, waits for them, and re-layouts  26.4 us (7%)
    pallas_call x1, Pallas kernels, on_device(): pl.pallas_call(functools.partial(kernel, n_dp, n_ten, width), out_shape=(...  346 us
    unnamed x17, local copies, waits for them, and re-layouts  24.7 us

profile of v5, /device:TPU:0, one launch (start us, length us, event | category | flops | bytes accessed | tf_op | source)
XLA Modules:
  0.0 372.9 jit_solution(1929918850804504459)
XLA Ops:
  0.6 3.0 copy.11
  3.6 1.8 copy.12
  5.4 345.7 %grad_update.1 = (f32[320,6656]{1,0:T(8,128)}, f32[320,6656]{1,0:T(8,128)}, f32[320,6656]{1,0:T(8,128)}, bf16[160,13312]{1,0:T(8,128)(2,1)}) custom-call(bf16[512,6656]{1,0:T(8,128)(2,1)} %gate.1, bf16[512,6656]{1,0:T(8,128)(2,1)} %up.1, bf16[4,640,512]{2,1,0:T(8,128)(2,1)} %bitcast.11, f32[320,6656]{1,0:T(8,128)} %master.1, f32[320,6656]{1,0:T(8,128)} %one.1, ...), custom_call_target="tpu_custom_call" | custom-call | flops 34896609280 | bytes 64749568 | tf_op jit(solution)/shard_map/grad_update/pallas_call | solution.py:480
  351.2 0.0 copy-start
  351.2 0.0 slice-start
  351.2 0.0 slice-start.1
  351.2 8.5 %copy.17 = f32[320,6656]{1,0:T(8,128)} copy(f32[320,6656]{1,0:T(8,128)} %get-tuple-element.8) | data formatting | bytes 17039360
  359.7 0.0 copy-done
  359.7 0.0 slice-start.2
  359.7 0.0 slice-start.3
  359.7 4.3 %copy.18 = f32[320,6656]{1,0:T(8,128)} copy(f32[320,6656]{1,0:T(8,128)S(1)} %copy-done) | data formatting | bytes 17039360
  364.0 0.0 slice-done
  364.0 1.6 slice-done.1
  365.6 0.0 slice-done.2
  365.6 0.0 slice-start.4
  365.6 4.3 %copy.19 = f32[320,6656]{1,0:T(8,128)} copy(f32[320,6656]{1,0:T(8,128)S(1)} %bitcast.8) | data formatting | bytes 17039360
  369.9 0.0 slice-done.3
  369.9 0.9 slice-done.4
  370.8 2.0 copy.20
  (2 shorter events, 0.0 us)
Async XLA Ops:
  351.2 8.5 %copy-start = (f32[320,6656]{1,0:T(8,128)S(1)}, f32[320,6656]{1,0:T(8,128)}, u32[]{:S(2)}) copy-start(f32[320,6656]{1,0:T(8,128)} %get-tuple-element.9) | copy-start | bytes 25559044
  351.2 12.8 %slice-start = ((s8[8519680]{0:T(1024)(128)(4,1)}), s8[4194304]{0:T(1024)(128)(4,1)S(1)}, s32[]{:S(2)}) async-start(s8[8519680]{0:T(1024)(128)(4,1)} %bitcast.7), calls=%async_computation | async-start | bytes 8388608
  351.2 14.4 %slice-start.1 = ((s8[8519680]{0:T(1024)(128)(4,1)}), s8[4194304]{0:T(1024)(128)(4,1)S(1)}, s32[]{:S(2)}) async-start(s8[8519680]{0:T(1024)(128)(4,1)} %bitcast.7), calls=%async_computation.1 | async-start | bytes 8388608
  359.7 5.9 %slice-start.2 = ((s8[8519680]{0:T(1024)(128)(4,1)}), s8[131072]{0:T(1024)(128)(4,1)S(1)}, s32[]{:S(2)}) async-start(s8[8519680]{0:T(1024)(128)(4,1)} %bitcast.7), calls=%async_computation.2 | async-start | bytes 262144
  359.7 10.2 %slice-start.3 = ((s8[4259840]{0:T(1024)(128)(4,1)}), s8[65536]{0:T(1024)(128)(4,1)S(1)}, s32[]{:S(2)}) async-start(s8[4259840]{0:T(1024)(128)(4,1)} %bitcast.9), calls=%async_computation.3 | async-start | bytes 131072
  365.6 5.3 %slice-start.4 = ((s8[4259840]{0:T(1024)(128)(4,1)}), s8[4194304]{0:T(1024)(128)(4,1)S(1)}, s32[]{:S(2)}) async-start(s8[4259840]{0:T(1024)(128)(4,1)} %bitcast.9), calls=%async_computation.4 | async-start | bytes 8388608
